TPU v7x, 32 devices: a whole 2x2x4 slice. The times are simulated.
32 devices in a mesh: tm: 8 (over z, x), phase: 4 (over y, core).
Axes of the slice: x: 2, y: 2, z: 4, core: 2. Of those that a mesh axis runs over, the one named last changes fastest.
Arguments:
- frames: bfloat16 [2, 1024, 1024], P(None, 'tm'), may hold values from -6 to 6
- frame_counts: int32 [2, 32], replicated, may hold values from 1 to 32, as said below
- w_query: bfloat16 [4, 1024, 1024], P('phase')
- w_key: bfloat16 [4, 1024, 1024], P('phase')
- w_value: bfloat16 [4, 1024, 1024], P('phase'), may hold values from -0.1875 to 0.1875
- w_out: bfloat16 [4, 1024, 1024], P('phase'), may hold values from -0.1875 to 0.1875
- conv_kernel: bfloat16 [4, 31, 1024], P('phase'), may hold values from -1 to 1
- w_point: bfloat16 [4, 1024, 1024], P('phase'), may hold values from -0.1875 to 0.1875
Outputs:
- layer_outputs: bfloat16 [4, 2, 1024, 1024], P('phase', None, 'tm')
Inputs may be any that keep to these rules, and one draw needn't show every extreme that they name: `frame_counts`: A segment's valid frames are its first ones; the largest count 32 occurs in every draw.
All inputs are finite; a program needn't handle non-finite values.
Results may differ from a plain program's by a relative error of at most 0.034.
Values may be sent and summed in bfloat16 or wider, within the bound.
No kernel may reach another device: no remote copies, remote signals or barrier semaphores. Data moves between devices by JAX's collectives and lax.ppermute only.
A program may use at most 64 MiB of HBM per device.

v0:
```python
import math

import jax
import jax.numpy as jnp
from jax import lax
from jax.sharding import PartitionSpec as P

HEADS = 16
SEG = 32
LC = 64
NMEM = 4
KW = 31
SEG_MB = 4


EPSILON = 1e-05


def from_behind(block, axis, distance):
    devices = range(lax.axis_size(axis))
    route = [((i - distance) % len(devices), i) for i in devices]
    return lax.ppermute(block, axis, route)


def passed_along(block, axis, distance):
    devices = range(lax.axis_size(axis))
    route = [(i - distance, i) for i in devices if i - distance in devices]
    return lax.ppermute(block, axis, route)


def layer_norm(values):
    center = values - jnp.mean(values, axis=-1, keepdims=True)
    spread = jnp.mean(center * center, axis=-1, keepdims=True)
    return center * lax.rsqrt(spread + EPSILON)


def attend_blocks(queries, blocks):
    query_len, model_width = queries.shape
    head_dim = model_width // HEADS
    split_q = queries.reshape(query_len, HEADS, head_dim)
    score_list = []
    for key_rows, value_rows, allowed in blocks:
        split_k = key_rows.reshape(key_rows.shape[0], HEADS, head_dim)
        scores = jnp.einsum(
            "qhd,khd->hqk", split_q, split_k, preferred_element_type=jnp.float32
        ) / math.sqrt(head_dim)
        score_list.append(jnp.where(allowed[None, :, :], scores, -1e30))
    top_score = score_list[0].max(axis=-1, keepdims=True)
    for scores in score_list[1:]:
        top_score = jnp.maximum(top_score, scores.max(axis=-1, keepdims=True))
    exp_list = [jnp.exp(scores - top_score) for scores in score_list]
    total = exp_list[0].sum(axis=-1, keepdims=True)
    for exponent in exp_list[1:]:
        total = total + exponent.sum(axis=-1, keepdims=True)
    context = jnp.zeros((query_len, HEADS, head_dim), jnp.float32)
    for exponent, block in zip(exp_list, blocks):
        weights = (exponent / total).astype(jnp.bfloat16)
        split_v = block[1].reshape(block[1].shape[0], HEADS, head_dim)
        context = context + jnp.einsum(
            "hqk,khd->qhd", weights, split_v, preferred_element_type=jnp.float32
        )
    return context.reshape(query_len, model_width)


def settle(received, stashed, leading):
    return jax.tree.map(
        lambda current, earlier: jnp.where(leading, earlier, current), received, stashed
    )


def project(rows_in, weight):
    return jnp.dot(rows_in, weight, preferred_element_type=jnp.float32).astype(jnp.bfloat16)


def per_device(frames, frame_counts, w_query, w_key, w_value, w_out, conv_kernel, w_point):
    micro_count, row_count, model_width = frames.shape
    phase_count = lax.axis_size("phase")
    shard_count = lax.axis_size("tm")
    phase_id = lax.axis_index("phase")
    shard_id = lax.axis_index("tm")
    query_weight = w_query[0]
    key_weight = w_key[0]
    value_weight = w_value[0]
    out_weight = w_out[0]
    kernel = conv_kernel[0].astype(jnp.float32)
    point_weight = w_point[0]
    padded_counts = jnp.concatenate([jnp.zeros((SEG_MB,), jnp.int32), frame_counts.reshape(-1)])
    leading = shard_id == 0
    own_index = jnp.arange(row_count, dtype=jnp.int32)
    left_index = jnp.arange(LC, dtype=jnp.int32)
    slot_index = jnp.arange(2 * SEG_MB, dtype=jnp.int32)
    frame_segment = own_index // SEG
    block_segment = jnp.arange(SEG_MB, dtype=jnp.int32)

    def masks(segment_ids, own_valid, left_valid, slot_live):
        first_frame = segment_ids[:, None] * SEG
        own_ok = (
            (own_index[None, :] >= first_frame - LC)
            & (own_index[None, :] < first_frame + SEG)
            & own_valid[None, :]
        )
        left_ok = (left_index[None, :] - LC >= first_frame - LC) & left_valid[None, :]
        slot_ok = (
            (slot_index[None, :] >= segment_ids[:, None] + SEG_MB - NMEM)
            & (slot_index[None, :] < segment_ids[:, None] + SEG_MB)
            & slot_live[None, :]
        )
        return (own_ok, left_ok, slot_ok)

    def empty_rows(count):
        return jnp.zeros((count, model_width), jnp.bfloat16)

    context_init = (empty_rows(LC), empty_rows(LC))
    memory_init = (empty_rows(SEG_MB), empty_rows(SEG_MB))

    def one_step(step_index, state_tuple):
        inbox, context_stash, memory_stash, rim_stash, outputs = state_tuple
        position = step_index - phase_id
        active = (position >= 0) & (position < micro_count)
        clipped = jnp.clip(position, 0, micro_count - 1)
        own_input = lax.dynamic_index_in_dim(frames, clipped, 0, keepdims=False)
        layer_input = jnp.where(phase_id == 0, own_input, inbox)
        first_segment = clipped * (shard_count * SEG_MB) + shard_id * SEG_MB
        near_counts = lax.dynamic_slice_in_dim(padded_counts, first_segment, 2 * SEG_MB)
        frame_mask = jnp.arange(SEG, dtype=jnp.int32)[None, :] < near_counts[:, None]
        own_valid = frame_mask[SEG_MB:].reshape(-1)
        left_valid = frame_mask[:SEG_MB].reshape(-1)[SEG_MB * SEG - LC :]
        slot_live = near_counts > 0
        row_mask = own_valid.astype(jnp.float32).reshape(row_count, 1)
        inputs = layer_input.astype(jnp.float32)
        normed = layer_norm(inputs).astype(jnp.bfloat16)
        queries = project(normed, query_weight)
        key_own = project(normed, key_weight)
        value_own = project(normed, value_weight)
        received = from_behind((key_own[row_count - LC :], value_own[row_count - LC :]), "tm", 1)
        key_left, value_left = settle(received, context_stash, leading)
        seg_rows = normed.reshape(SEG_MB, SEG, model_width).astype(jnp.float32)
        own_mask = frame_mask[SEG_MB:].astype(jnp.float32)
        own_counts = near_counts[SEG_MB:].astype(jnp.float32)
        summary = (jnp.sum(seg_rows * own_mask[:, :, None], axis=1) / own_counts[:, None]).astype(
            jnp.bfloat16
        )
        summary_q = project(summary, query_weight)
        sum_own_ok, sum_left_ok, unused_ok = masks(block_segment, own_valid, left_valid, slot_live)
        memory = attend_blocks(
            summary_q, [(key_left, value_left, sum_left_ok), (key_own, value_own, sum_own_ok)]
        ).astype(jnp.bfloat16)
        mem_key_own = project(memory, key_weight)
        mem_value_own = project(memory, value_weight)
        received_mem = from_behind((mem_key_own, mem_value_own), "tm", 1)
        mem_key_prev, mem_value_prev = settle(received_mem, memory_stash, leading)
        own_ok, left_ok, slot_ok = masks(frame_segment, own_valid, left_valid, slot_live)
        context = attend_blocks(
            queries,
            [
                (mem_key_prev, mem_value_prev, slot_ok[:, :SEG_MB]),
                (mem_key_own, mem_value_own, slot_ok[:, SEG_MB:]),
                (key_left, value_left, left_ok),
                (key_own, value_own, own_ok),
            ],
        )
        context = context.astype(jnp.bfloat16)
        residual = (
            inputs + jnp.dot(context, out_weight, preferred_element_type=jnp.float32)
        ).astype(jnp.bfloat16)
        conv_in = (layer_norm(residual.astype(jnp.float32)) * row_mask).astype(jnp.bfloat16)
        received_rim = from_behind(conv_in[row_count - (KW - 1) :], "tm", 1)
        rim_rows = jnp.where(leading, rim_stash, received_rim)
        rim_rows = jnp.where(leading & (clipped == 0), jnp.zeros_like(rim_rows), rim_rows)
        extended = jnp.concatenate([rim_rows, conv_in])
        depth = jnp.zeros((row_count, model_width), jnp.float32)
        for offset in range(KW):
            depth = depth + kernel[offset] * extended[offset : offset + row_count].astype(
                jnp.float32
            )
        gated = jax.nn.silu(layer_norm(depth)).astype(jnp.bfloat16)
        mixed = residual.astype(jnp.float32) + jnp.dot(
            gated, point_weight, preferred_element_type=jnp.float32
        )
        result = (mixed * row_mask).astype(jnp.bfloat16)
        existing = lax.dynamic_index_in_dim(outputs, clipped, 0, keepdims=False)
        outputs = lax.dynamic_update_index_in_dim(
            outputs, jnp.where(active, result, existing), clipped, 0
        )
        next_inbox = passed_along(result, "phase", 1)
        return (next_inbox, received, received_mem, received_rim, outputs)

    start_state = (
        empty_rows(row_count),
        context_init,
        memory_init,
        empty_rows(KW - 1),
        jnp.zeros((micro_count, row_count, model_width), jnp.bfloat16),
    )
    final_state = lax.fori_loop(0, micro_count + phase_count - 1, one_step, start_state)
    return final_state[4][None]


def solution(mesh):
    in_specs = (
        P(None, "tm", None),
        P(),
        P("phase", None, None),
        P("phase", None, None),
        P("phase", None, None),
        P("phase", None, None),
        P("phase", None, None),
        P("phase", None, None),
    )
    out_specs = P("phase", None, "tm", None)
    return jax.shard_map(
        per_device, mesh=mesh, in_specs=in_specs, out_specs=out_specs, check_vma=False
    )
```

profile of v0, /device:TPU:1, one launch (start us, length us, event | category | flops | bytes accessed | tf_op | source)
XLA Modules:
  0.0 386.8 jit_solution(14565276080577112635)
XLA Ops:
  6.9 379.8 %while.32 = (s32[]{:T(128)}, bf16[128,1024]{1,0:T(8,128)(2,1)S(1)}, bf16[64,1024]{1,0:T(8,128)(2,1)}, bf16[64,1024]{1,0:T(8,128)(2,1)}, bf16[4,1024]{1,0:T(4,128...) while((s32[]{:T(128)}, bf16[128,1024]{1,0:T(8,128)(2,1)S(1)}, ...), condition=%wide.region_20.21_spmd.clone.clone, body=%wide.region_0.20_spmd.clone.clone.sunk | while | flops 1509182336 | bytes 101471064 | solution.py:195
  10.7 2.0 convolution_convert_fusion.14
  13.4 2.0 collective-permute-start
  33.9 2.0 convolution_convert_fusion.13
  58.4 2.2 collective-permute-done.2
  66.0 5.8 %collective-permute-done.4 = bf16[30,1024]{1,0:T(8,128)(2,1)S(1)} collective-permute-done((bf16[30,1024]{1,0:T(8,128)(2,1)S(1)}, bf16[30,1024]{1,0:T(8,128)(2,1)S(1)}, u32[]{:S(2)}, u32[]{:S(2)}) %collective-permute-start.4) | collective-permute-done | bytes 61472 | tf_op jit(solution)/shard_map/while/body/eval_jaxpr/ppermute | solution.py:22
  72.1 2.5 fusion.246
  75.4 6.6 %collective-permute-start.5 = (bf16[128,1024]{1,0:T(8,128)(2,1)S(1)}, bf16[128,1024]{1,0:T(8,128)(2,1)S(1)}, u32[]{:S(2)}, u32[]{:S(2)}) collective-permute-start(bf16[128,1024]{1,0:T(8,128)(2,1)S(1)} %get-tuple-element.1277), channel_id=1, source_target_pairs={{0,1},{1,2},{2,3},{4,5},{5,6},{6,7},{8,9},{9,10},{10,11},{12,13},{... | collective-permute-start | bytes 786440 | tf_op jit(solution)/shard_map/while/body/eval_jaxpr/ppermute | solution.py:28
  89.8 2.0 convolution_convert_fusion.14
  133.0 3.3 collective-permute-done.2
  141.8 6.5 %collective-permute-done.4 = bf16[30,1024]{1,0:T(8,128)(2,1)S(1)} collective-permute-done((bf16[30,1024]{1,0:T(8,128)(2,1)S(1)}, bf16[30,1024]{1,0:T(8,128)(2,1)S(1)}, u32[]{:S(2)}, u32[]{:S(2)}) %collective-permute-start.4) | collective-permute-done | bytes 61472 | tf_op jit(solution)/shard_map/while/body/eval_jaxpr/ppermute | solution.py:22
  148.6 2.5 fusion.246
  152.0 5.2 %collective-permute-start.5 = (bf16[128,1024]{1,0:T(8,128)(2,1)S(1)}, bf16[128,1024]{1,0:T(8,128)(2,1)S(1)}, u32[]{:S(2)}, u32[]{:S(2)}) collective-permute-start(bf16[128,1024]{1,0:T(8,128)(2,1)S(1)} %get-tuple-element.1277), channel_id=1, source_target_pairs={{0,1},{1,2},{2,3},{4,5},{5,6},{6,7},{8,9},{9,10},{10,11},{12,13},{... | collective-permute-start | bytes 786440 | tf_op jit(solution)/shard_map/while/body/eval_jaxpr/ppermute | solution.py:28
  164.9 2.0 convolution_convert_fusion.14
  184.9 2.0 convolution_convert_fusion.13
  206.4 2.1 collective-permute-start.3
  208.9 2.6 collective-permute-done.2
  217.0 5.8 %collective-permute-done.4 = bf16[30,1024]{1,0:T(8,128)(2,1)S(1)} collective-permute-done((bf16[30,1024]{1,0:T(8,128)(2,1)S(1)}, bf16[30,1024]{1,0:T(8,128)(2,1)S(1)}, u32[]{:S(2)}, u32[]{:S(2)}) %collective-permute-start.4) | collective-permute-done | bytes 61472 | tf_op jit(solution)/shard_map/while/body/eval_jaxpr/ppermute | solution.py:22
  223.0 2.5 fusion.246
  226.4 5.9 %collective-permute-start.5 = (bf16[128,1024]{1,0:T(8,128)(2,1)S(1)}, bf16[128,1024]{1,0:T(8,128)(2,1)S(1)}, u32[]{:S(2)}, u32[]{:S(2)}) collective-permute-start(bf16[128,1024]{1,0:T(8,128)(2,1)S(1)} %get-tuple-element.1277), channel_id=1, source_target_pairs={{0,1},{1,2},{2,3},{4,5},{5,6},{6,7},{8,9},{9,10},{10,11},{12,13},{... | collective-permute-start | bytes 786440 | tf_op jit(solution)/shard_map/while/body/eval_jaxpr/ppermute | solution.py:28
  240.1 2.0 convolution_convert_fusion.14
  281.6 2.5 collective-permute-start.3
  284.5 2.2 collective-permute-done.2
  292.1 5.8 %collective-permute-done.4 = bf16[30,1024]{1,0:T(8,128)(2,1)S(1)} collective-permute-done((bf16[30,1024]{1,0:T(8,128)(2,1)S(1)}, bf16[30,1024]{1,0:T(8,128)(2,1)S(1)}, u32[]{:S(2)}, u32[]{:S(2)}) %collective-permute-start.4) | collective-permute-done | bytes 61472 | tf_op jit(solution)/shard_map/while/body/eval_jaxpr/ppermute | solution.py:22
  298.2 2.5 fusion.246
  301.6 5.9 %collective-permute-start.5 = (bf16[128,1024]{1,0:T(8,128)(2,1)S(1)}, bf16[128,1024]{1,0:T(8,128)(2,1)S(1)}, u32[]{:S(2)}, u32[]{:S(2)}) collective-permute-start(bf16[128,1024]{1,0:T(8,128)(2,1)S(1)} %get-tuple-element.1277), channel_id=1, source_target_pairs={{0,1},{1,2},{2,3},{4,5},{5,6},{6,7},{8,9},{9,10},{10,11},{12,13},{... | collective-permute-start | bytes 786440 | tf_op jit(solution)/shard_map/while/body/eval_jaxpr/ppermute | solution.py:28
  315.3 2.0 convolution_convert_fusion.14
  356.8 2.5 collective-permute-start.3
  359.7 2.2 collective-permute-done.2
  367.3 5.8 %collective-permute-done.4 = bf16[30,1024]{1,0:T(8,128)(2,1)S(1)} collective-permute-done((bf16[30,1024]{1,0:T(8,128)(2,1)S(1)}, bf16[30,1024]{1,0:T(8,128)(2,1)S(1)}, u32[]{:S(2)}, u32[]{:S(2)}) %collective-permute-start.4) | collective-permute-done | bytes 61472 | tf_op jit(solution)/shard_map/while/body/eval_jaxpr/ppermute | solution.py:22
  373.4 2.5 fusion.246
  376.8 5.9 %collective-permute-start.5 = (bf16[128,1024]{1,0:T(8,128)(2,1)S(1)}, bf16[128,1024]{1,0:T(8,128)(2,1)S(1)}, u32[]{:S(2)}, u32[]{:S(2)}) collective-permute-start(bf16[128,1024]{1,0:T(8,128)(2,1)S(1)} %get-tuple-element.1277), channel_id=1, source_target_pairs={{0,1},{1,2},{2,3},{4,5},{5,6},{6,7},{8,9},{9,10},{10,11},{12,13},{... | collective-permute-start | bytes 786440 | tf_op jit(solution)/shard_map/while/body/eval_jaxpr/ppermute | solution.py:28
  (1059 shorter events, 274.6 us)
Async XLA Ops:
  13.4 28.6 %collective-permute-start = (bf16[64,1024]{1,0:T(8,128)(2,1)}, bf16[64,1024]{1,0:T(8,128)(2,1)S(1)}, u32[]{:S(2)}, u32[]{:S(2)}) collective-permute-start(bf16[64,1024]{1,0:T(8,128)(2,1)} %slice.1567), channel_id=1, source_target_pairs={{28,0},{0,4},{4,8},{8,12},{12,16},{16,20},{20,24},{24,28},{29,1},{... | collective-permute-start | bytes 393224 | tf_op jit(solution)/shard_map/while/body/eval_jaxpr/ppermute | solution.py:22
  16.5 31.6 %collective-permute-start.1 = (bf16[64,1024]{1,0:T(8,128)(2,1)}, bf16[64,1024]{1,0:T(8,128)(2,1)}, u32[]{:S(2)}, u32[]{:S(2)}) collective-permute-start(bf16[64,1024]{1,0:T(8,128)(2,1)} %slice.1569), channel_id=1, source_target_pairs={{28,0},{0,4},{4,8},{8,12},{12,16},{16,20},{20,24},{24,28},{29,1},{... | collective-permute-start | bytes 393224 | tf_op jit(solution)/shard_map/while/body/eval_jaxpr/ppermute | solution.py:22
  26.3 11.1 %copy-start.3 = (bf16[128,1024]{0,1:T(8,128)(2,1)}, bf16[128,1024]{0,1:T(8,128)(2,1)S(1)}, u32[]{:S(2)}) copy-start(bf16[128,1024]{0,1:T(8,128)(2,1)S(1)} %copy.96) | copy-start | bytes 786436 | tf_op jit(solution)/shard_map/while
  55.3 5.2 %collective-permute-start.2 = (bf16[4,1024]{1,0:T(4,128)(2,1)S(1)}, bf16[4,1024]{1,0:T(4,128)(2,1)S(1)}, u32[]{:S(2)}, u32[]{:S(2)}) collective-permute-start(bf16[4,1024]{1,0:T(4,128)(2,1)S(1)} %convolution_convert_fusion.16), channel_id=1, source_target_pairs={{28,0},{0,4},{4,8},{8,12},{12,16},{16,20},{20,24},{24,28},{29,1},{... | collective-permute-start | bytes 24584 | tf_op jit(solution)/shard_map/while/body/eval_jaxpr/ppermute | solution.py:22
  56.6 7.2 %collective-permute-start.3 = (bf16[4,1024]{1,0:T(4,128)(2,1)S(1)}, bf16[4,1024]{1,0:T(4,128)(2,1)S(1)}, u32[]{:S(2)}, u32[]{:S(2)}) collective-permute-start(bf16[4,1024]{1,0:T(4,128)(2,1)S(1)} %convolution_convert_fusion.17), channel_id=1, source_target_pairs={{28,0},{0,4},{4,8},{8,12},{12,16},{16,20},{20,24},{24,28},{29,1},{... | collective-permute-start | bytes 24584 | tf_op jit(solution)/shard_map/while/body/eval_jaxpr/ppermute | solution.py:22
  65.9 5.9 %collective-permute-start.4 = (bf16[30,1024]{1,0:T(8,128)(2,1)S(1)}, bf16[30,1024]{1,0:T(8,128)(2,1)S(1)}, u32[]{:S(2)}, u32[]{:S(2)}) collective-permute-start(bf16[30,1024]{1,0:T(8,128)(2,1)S(1)} %slice.1570), channel_id=1, source_target_pairs={{28,0},{0,4},{4,8},{8,12},{12,16},{16,20},{20,24},{24,28},{29,1},{... | collective-permute-start | bytes 184328 | tf_op jit(solution)/shard_map/while/body/eval_jaxpr/ppermute | solution.py:22
  75.4 10.6 %collective-permute-start.5 = (bf16[128,1024]{1,0:T(8,128)(2,1)S(1)}, bf16[128,1024]{1,0:T(8,128)(2,1)S(1)}, u32[]{:S(2)}, u32[]{:S(2)}) collective-permute-start(bf16[128,1024]{1,0:T(8,128)(2,1)S(1)} %get-tuple-element.1277), channel_id=1, source_target_pairs={{0,1},{1,2},{2,3},{4,5},{5,6},{6,7},{8,9},{9,10},{10,11},{12,13},{... | collective-permute-start | bytes 786440 | tf_op jit(solution)/shard_map/while/body/eval_jaxpr/ppermute | solution.py:28
  92.5 25.3 %collective-permute-start = (bf16[64,1024]{1,0:T(8,128)(2,1)}, bf16[64,1024]{1,0:T(8,128)(2,1)S(1)}, u32[]{:S(2)}, u32[]{:S(2)}) collective-permute-start(bf16[64,1024]{1,0:T(8,128)(2,1)} %slice.1567), channel_id=1, source_target_pairs={{28,0},{0,4},{4,8},{8,12},{12,16},{16,20},{20,24},{24,28},{29,1},{... | collective-permute-start | bytes 393224 | tf_op jit(solution)/shard_map/while/body/eval_jaxpr/ppermute | solution.py:22
  93.6 30.3 %collective-permute-start.1 = (bf16[64,1024]{1,0:T(8,128)(2,1)}, bf16[64,1024]{1,0:T(8,128)(2,1)}, u32[]{:S(2)}, u32[]{:S(2)}) collective-permute-start(bf16[64,1024]{1,0:T(8,128)(2,1)} %slice.1569), channel_id=1, source_target_pairs={{28,0},{0,4},{4,8},{8,12},{12,16},{16,20},{20,24},{24,28},{29,1},{... | collective-permute-start | bytes 393224 | tf_op jit(solution)/shard_map/while/body/eval_jaxpr/ppermute | solution.py:22
  102.1 11.1 %copy-start.3 = (bf16[128,1024]{0,1:T(8,128)(2,1)}, bf16[128,1024]{0,1:T(8,128)(2,1)S(1)}, u32[]{:S(2)}) copy-start(bf16[128,1024]{0,1:T(8,128)(2,1)S(1)} %copy.96) | copy-start | bytes 786436 | tf_op jit(solution)/shard_map/while
  131.1 5.2 %collective-permute-start.2 = (bf16[4,1024]{1,0:T(4,128)(2,1)S(1)}, bf16[4,1024]{1,0:T(4,128)(2,1)S(1)}, u32[]{:S(2)}, u32[]{:S(2)}) collective-permute-start(bf16[4,1024]{1,0:T(4,128)(2,1)S(1)} %convolution_convert_fusion.16), channel_id=1, source_target_pairs={{28,0},{0,4},{4,8},{8,12},{12,16},{16,20},{20,24},{24,28},{29,1},{... | collective-permute-start | bytes 24584 | tf_op jit(solution)/shard_map/while/body/eval_jaxpr/ppermute | solution.py:22
  131.2 8.4 %collective-permute-start.3 = (bf16[4,1024]{1,0:T(4,128)(2,1)S(1)}, bf16[4,1024]{1,0:T(4,128)(2,1)S(1)}, u32[]{:S(2)}, u32[]{:S(2)}) collective-permute-start(bf16[4,1024]{1,0:T(4,128)(2,1)S(1)} %convolution_convert_fusion.17), channel_id=1, source_target_pairs={{28,0},{0,4},{4,8},{8,12},{12,16},{16,20},{20,24},{24,28},{29,1},{... | collective-permute-start | bytes 24584 | tf_op jit(solution)/shard_map/while/body/eval_jaxpr/ppermute | solution.py:22
  141.7 6.6 %collective-permute-start.4 = (bf16[30,1024]{1,0:T(8,128)(2,1)S(1)}, bf16[30,1024]{1,0:T(8,128)(2,1)S(1)}, u32[]{:S(2)}, u32[]{:S(2)}) collective-permute-start(bf16[30,1024]{1,0:T(8,128)(2,1)S(1)} %slice.1570), channel_id=1, source_target_pairs={{28,0},{0,4},{4,8},{8,12},{12,16},{16,20},{20,24},{24,28},{29,1},{... | collective-permute-start | bytes 184328 | tf_op jit(solution)/shard_map/while/body/eval_jaxpr/ppermute | solution.py:22
  152.0 9.2 %collective-permute-start.5 = (bf16[128,1024]{1,0:T(8,128)(2,1)S(1)}, bf16[128,1024]{1,0:T(8,128)(2,1)S(1)}, u32[]{:S(2)}, u32[]{:S(2)}) collective-permute-start(bf16[128,1024]{1,0:T(8,128)(2,1)S(1)} %get-tuple-element.1277), channel_id=1, source_target_pairs={{0,1},{1,2},{2,3},{4,5},{5,6},{6,7},{8,9},{9,10},{10,11},{12,13},{... | collective-permute-start | bytes 786440 | tf_op jit(solution)/shard_map/while/body/eval_jaxpr/ppermute | solution.py:28
  167.6 25.3 %collective-permute-start = (bf16[64,1024]{1,0:T(8,128)(2,1)}, bf16[64,1024]{1,0:T(8,128)(2,1)S(1)}, u32[]{:S(2)}, u32[]{:S(2)}) collective-permute-start(bf16[64,1024]{1,0:T(8,128)(2,1)} %slice.1567), channel_id=1, source_target_pairs={{28,0},{0,4},{4,8},{8,12},{12,16},{16,20},{20,24},{24,28},{29,1},{... | collective-permute-start | bytes 393224 | tf_op jit(solution)/shard_map/while/body/eval_jaxpr/ppermute | solution.py:22
  168.8 30.3 %collective-permute-start.1 = (bf16[64,1024]{1,0:T(8,128)(2,1)}, bf16[64,1024]{1,0:T(8,128)(2,1)}, u32[]{:S(2)}, u32[]{:S(2)}) collective-permute-start(bf16[64,1024]{1,0:T(8,128)(2,1)} %slice.1569), channel_id=1, source_target_pairs={{28,0},{0,4},{4,8},{8,12},{12,16},{16,20},{20,24},{24,28},{29,1},{... | collective-permute-start | bytes 393224 | tf_op jit(solution)/shard_map/while/body/eval_jaxpr/ppermute | solution.py:22
  206.3 5.2 %collective-permute-start.2 = (bf16[4,1024]{1,0:T(4,128)(2,1)S(1)}, bf16[4,1024]{1,0:T(4,128)(2,1)S(1)}, u32[]{:S(2)}, u32[]{:S(2)}) collective-permute-start(bf16[4,1024]{1,0:T(4,128)(2,1)S(1)} %convolution_convert_fusion.16), channel_id=1, source_target_pairs={{28,0},{0,4},{4,8},{8,12},{12,16},{16,20},{20,24},{24,28},{29,1},{... | collective-permute-start | bytes 24584 | tf_op jit(solution)/shard_map/while/body/eval_jaxpr/ppermute | solution.py:22
  206.4 8.4 %collective-permute-start.3 = (bf16[4,1024]{1,0:T(4,128)(2,1)S(1)}, bf16[4,1024]{1,0:T(4,128)(2,1)S(1)}, u32[]{:S(2)}, u32[]{:S(2)}) collective-permute-start(bf16[4,1024]{1,0:T(4,128)(2,1)S(1)} %convolution_convert_fusion.17), channel_id=1, source_target_pairs={{28,0},{0,4},{4,8},{8,12},{12,16},{16,20},{20,24},{24,28},{29,1},{... | collective-permute-start | bytes 24584 | tf_op jit(solution)/shard_map/while/body/eval_jaxpr/ppermute | solution.py:22
  216.8 5.9 %collective-permute-start.4 = (bf16[30,1024]{1,0:T(8,128)(2,1)S(1)}, bf16[30,1024]{1,0:T(8,128)(2,1)S(1)}, u32[]{:S(2)}, u32[]{:S(2)}) collective-permute-start(bf16[30,1024]{1,0:T(8,128)(2,1)S(1)} %slice.1570), channel_id=1, source_target_pairs={{28,0},{0,4},{4,8},{8,12},{12,16},{16,20},{20,24},{24,28},{29,1},{... | collective-permute-start | bytes 184328 | tf_op jit(solution)/shard_map/while/body/eval_jaxpr/ppermute | solution.py:22
  226.4 10.0 %collective-permute-start.5 = (bf16[128,1024]{1,0:T(8,128)(2,1)S(1)}, bf16[128,1024]{1,0:T(8,128)(2,1)S(1)}, u32[]{:S(2)}, u32[]{:S(2)}) collective-permute-start(bf16[128,1024]{1,0:T(8,128)(2,1)S(1)} %get-tuple-element.1277), channel_id=1, source_target_pairs={{0,1},{1,2},{2,3},{4,5},{5,6},{6,7},{8,9},{9,10},{10,11},{12,13},{... | collective-permute-start | bytes 786440 | tf_op jit(solution)/shard_map/while/body/eval_jaxpr/ppermute | solution.py:28
  242.8 25.3 %collective-permute-start = (bf16[64,1024]{1,0:T(8,128)(2,1)}, bf16[64,1024]{1,0:T(8,128)(2,1)S(1)}, u32[]{:S(2)}, u32[]{:S(2)}) collective-permute-start(bf16[64,1024]{1,0:T(8,128)(2,1)} %slice.1567), channel_id=1, source_target_pairs={{28,0},{0,4},{4,8},{8,12},{12,16},{16,20},{20,24},{24,28},{29,1},{... | collective-permute-start | bytes 393224 | tf_op jit(solution)/shard_map/while/body/eval_jaxpr/ppermute | solution.py:22
  244.0 30.3 %collective-permute-start.1 = (bf16[64,1024]{1,0:T(8,128)(2,1)}, bf16[64,1024]{1,0:T(8,128)(2,1)}, u32[]{:S(2)}, u32[]{:S(2)}) collective-permute-start(bf16[64,1024]{1,0:T(8,128)(2,1)} %slice.1569), channel_id=1, source_target_pairs={{28,0},{0,4},{4,8},{8,12},{12,16},{16,20},{20,24},{24,28},{29,1},{... | collective-permute-start | bytes 393224 | tf_op jit(solution)/shard_map/while/body/eval_jaxpr/ppermute | solution.py:22
  281.5 5.2 %collective-permute-start.2 = (bf16[4,1024]{1,0:T(4,128)(2,1)S(1)}, bf16[4,1024]{1,0:T(4,128)(2,1)S(1)}, u32[]{:S(2)}, u32[]{:S(2)}) collective-permute-start(bf16[4,1024]{1,0:T(4,128)(2,1)S(1)} %convolution_convert_fusion.16), channel_id=1, source_target_pairs={{28,0},{0,4},{4,8},{8,12},{12,16},{16,20},{20,24},{24,28},{29,1},{... | collective-permute-start | bytes 24584 | tf_op jit(solution)/shard_map/while/body/eval_jaxpr/ppermute | solution.py:22
  281.6 8.4 %collective-permute-start.3 = (bf16[4,1024]{1,0:T(4,128)(2,1)S(1)}, bf16[4,1024]{1,0:T(4,128)(2,1)S(1)}, u32[]{:S(2)}, u32[]{:S(2)}) collective-permute-start(bf16[4,1024]{1,0:T(4,128)(2,1)S(1)} %convolution_convert_fusion.17), channel_id=1, source_target_pairs={{28,0},{0,4},{4,8},{8,12},{12,16},{16,20},{20,24},{24,28},{29,1},{... | collective-permute-start | bytes 24584 | tf_op jit(solution)/shard_map/while/body/eval_jaxpr/ppermute | solution.py:22
  292.0 5.9 %collective-permute-start.4 = (bf16[30,1024]{1,0:T(8,128)(2,1)S(1)}, bf16[30,1024]{1,0:T(8,128)(2,1)S(1)}, u32[]{:S(2)}, u32[]{:S(2)}) collective-permute-start(bf16[30,1024]{1,0:T(8,128)(2,1)S(1)} %slice.1570), channel_id=1, source_target_pairs={{28,0},{0,4},{4,8},{8,12},{12,16},{16,20},{20,24},{24,28},{29,1},{... | collective-permute-start | bytes 184328 | tf_op jit(solution)/shard_map/while/body/eval_jaxpr/ppermute | solution.py:22
  301.6 10.0 %collective-permute-start.5 = (bf16[128,1024]{1,0:T(8,128)(2,1)S(1)}, bf16[128,1024]{1,0:T(8,128)(2,1)S(1)}, u32[]{:S(2)}, u32[]{:S(2)}) collective-permute-start(bf16[128,1024]{1,0:T(8,128)(2,1)S(1)} %get-tuple-element.1277), channel_id=1, source_target_pairs={{0,1},{1,2},{2,3},{4,5},{5,6},{6,7},{8,9},{9,10},{10,11},{12,13},{... | collective-permute-start | bytes 786440 | tf_op jit(solution)/shard_map/while/body/eval_jaxpr/ppermute | solution.py:28
  318.0 25.3 %collective-permute-start = (bf16[64,1024]{1,0:T(8,128)(2,1)}, bf16[64,1024]{1,0:T(8,128)(2,1)S(1)}, u32[]{:S(2)}, u32[]{:S(2)}) collective-permute-start(bf16[64,1024]{1,0:T(8,128)(2,1)} %slice.1567), channel_id=1, source_target_pairs={{28,0},{0,4},{4,8},{8,12},{12,16},{16,20},{20,24},{24,28},{29,1},{... | collective-permute-start | bytes 393224 | tf_op jit(solution)/shard_map/while/body/eval_jaxpr/ppermute | solution.py:22
  319.1 30.3 %collective-permute-start.1 = (bf16[64,1024]{1,0:T(8,128)(2,1)}, bf16[64,1024]{1,0:T(8,128)(2,1)}, u32[]{:S(2)}, u32[]{:S(2)}) collective-permute-start(bf16[64,1024]{1,0:T(8,128)(2,1)} %slice.1569), channel_id=1, source_target_pairs={{28,0},{0,4},{4,8},{8,12},{12,16},{16,20},{20,24},{24,28},{29,1},{... | collective-permute-start | bytes 393224 | tf_op jit(solution)/shard_map/while/body/eval_jaxpr/ppermute | solution.py:22
  356.7 5.2 %collective-permute-start.2 = (bf16[4,1024]{1,0:T(4,128)(2,1)S(1)}, bf16[4,1024]{1,0:T(4,128)(2,1)S(1)}, u32[]{:S(2)}, u32[]{:S(2)}) collective-permute-start(bf16[4,1024]{1,0:T(4,128)(2,1)S(1)} %convolution_convert_fusion.16), channel_id=1, source_target_pairs={{28,0},{0,4},{4,8},{8,12},{12,16},{16,20},{20,24},{24,28},{29,1},{... | collective-permute-start | bytes 24584 | tf_op jit(solution)/shard_map/while/body/eval_jaxpr/ppermute | solution.py:22
  356.8 8.4 %collective-permute-start.3 = (bf16[4,1024]{1,0:T(4,128)(2,1)S(1)}, bf16[4,1024]{1,0:T(4,128)(2,1)S(1)}, u32[]{:S(2)}, u32[]{:S(2)}) collective-permute-start(bf16[4,1024]{1,0:T(4,128)(2,1)S(1)} %convolution_convert_fusion.17), channel_id=1, source_target_pairs={{28,0},{0,4},{4,8},{8,12},{12,16},{16,20},{20,24},{24,28},{29,1},{... | collective-permute-start | bytes 24584 | tf_op jit(solution)/shard_map/while/body/eval_jaxpr/ppermute | solution.py:22
  367.2 5.9 %collective-permute-start.4 = (bf16[30,1024]{1,0:T(8,128)(2,1)S(1)}, bf16[30,1024]{1,0:T(8,128)(2,1)S(1)}, u32[]{:S(2)}, u32[]{:S(2)}) collective-permute-start(bf16[30,1024]{1,0:T(8,128)(2,1)S(1)} %slice.1570), channel_id=1, source_target_pairs={{28,0},{0,4},{4,8},{8,12},{12,16},{16,20},{20,24},{24,28},{29,1},{... | collective-permute-start | bytes 184328 | tf_op jit(solution)/shard_map/while/body/eval_jaxpr/ppermute | solution.py:22
  376.8 10.0 %collective-permute-start.5 = (bf16[128,1024]{1,0:T(8,128)(2,1)S(1)}, bf16[128,1024]{1,0:T(8,128)(2,1)S(1)}, u32[]{:S(2)}, u32[]{:S(2)}) collective-permute-start(bf16[128,1024]{1,0:T(8,128)(2,1)S(1)} %get-tuple-element.1277), channel_id=1, source_target_pairs={{0,1},{1,2},{2,3},{4,5},{5,6},{6,7},{8,9},{9,10},{10,11},{12,13},{... | collective-permute-start | bytes 786440 | tf_op jit(solution)/shard_map/while/body/eval_jaxpr/ppermute | solution.py:28
  (283 other events, 1717.0 us)
where the time goes:
time: 391 us; the launch traced here: 387 us
  other arithmetic  113 us (29%)
  local copies, waits for them, and re-layouts  94.5 us (24%)
  matrix products  88.7 us (23%)
  starting transfers between devices  44.1 us (11%)
  waiting for transfers between devices  42 us (11%)
  loops' own time  4.86 us (1%)
    ppermute x25, waiting for transfers between devices, from_behind(): return lax.ppermute(block, axis, route)  42 us
    while x595, local copies, waits for them, and re-layouts  30.5 us
    ppermute x5, starting transfers between devices, passed_along(): return lax.ppermute(block, axis, route)  29.6 us
    dot_general x30, matrix products, project(): jnp.dot(rows_in, weight, preferred_element_type=jnp.float32)  28.5 us
    dot_general x30, matrix products, attend_blocks(): jnp.einsum('hqk,khd->qhd', weights, split_v, preferred_element_type=jnp.f...  28.2 us
    dot_general x30, matrix products, attend_blocks(): jnp.einsum('qhd,khd->hqk', split_q, split_k, preferred_element_type=jnp.f...  26.2 us
    slice x10, local copies, waits for them, and re-layouts, one_step(): kernel[offset] * extended[offset:offset + row_count].astype(jnp.float32)  18.7 us
    reduce_sum x10, other arithmetic, layer_norm(): center = values - jnp.mean(values, axis=-1, keepdims=True)  18.7 us
  transfers between devices with their start and end apart: 30, of which 10 were waited for; matrix products, arithmetic and copies ran while one was open for 50% of the time, Pallas kernels for 0%

commit v1 on v0

v1 whole, which is shorter than its diff:
```python
import functools
import math

import jax
import jax.numpy as jnp
from jax import lax
from jax.experimental import pallas as pl
from jax.experimental.pallas import tpu as pltpu
from jax.sharding import PartitionSpec as P

HEADS = 16
SEG = 32
LC = 64
NMEM = 4
KW = 31

EPSILON = 1e-05
BACK = LC // SEG
HALO_SEGS = 1 + NMEM + BACK
HALO = HALO_SEGS * SEG
FAR = -1e30
OPEN = 3e38
TILE = 256
PAIR = 128


def layer_norm(values):
    center = values - jnp.mean(values, axis=-1, keepdims=True)
    spread = jnp.mean(center * center, axis=-1, keepdims=True)
    return center * lax.rsqrt(spread + EPSILON)


def dot(a, b):
    return jnp.dot(a, b, preferred_element_type=jnp.float32)


def dot_nt(a, b):
    return lax.dot_general(a, b, (((1,), (1,)), ((), ())), preferred_element_type=jnp.float32)


def halo_pieces(rows):
    pieces = []
    left = HALO
    while left > 0:
        take = min(rows, left)
        pieces.append((len(pieces) + 1, take))
        left -= take
    return pieces


def by_segment(index, counts, first, number):
    out = jnp.zeros(index.shape, jnp.int32)
    for s in range(number):
        out = jnp.where(index == s, counts[first + s], out)
    return out


def layer_kernel(cfg, *refs):
    rows, width, step, micro, phases, shards, segs_row, pieces = cfg
    refs = list(refs)
    meta, counts_ref = refs[:2]
    hbm_weights = refs[2:7]
    taps_hbm = refs[7]
    refs = refs[8:]
    count_p = len(pieces)
    with_frames = step < micro
    with_inbox = step >= 1
    with_prev = step >= 2
    if with_frames:
        frames_hbm, frame_halos = refs[0], refs[1 : 1 + count_p]
        refs = refs[1 + count_p :]
    if with_inbox:
        inbox, halos = refs[0], refs[1 : 1 + count_p]
        refs = refs[1 + count_p :]
    if with_prev:
        prevs = refs[:count_p]
        refs = refs[count_p:]
    if step >= 1:
        refs = refs[1:]
    outputs = refs[0]
    refs = refs[1:]
    with_relay = step < micro + phases - 2
    relays = []
    if with_relay:
        number = 1 + sum(1 for _, take in pieces if take < rows)
        relays = refs[:number]
        refs = refs[number:]
    (xe, normed, ke, ve, qe, ctx, res, cin, depth, gated, result, bias, mem_bias,
     wk, wv, wq, wo, wp, taps, wsem, xsem, osem) = refs

    ext = HALO + rows
    segs = ext // SEG
    q_rows = rows + SEG
    q_seg = HALO_SEGS - 1
    mem_first = q_seg - NMEM
    mems = segs - 1 - mem_first
    mem_pad = ke.shape[0] - ext
    key_seg = q_seg - BACK
    key_row = key_seg * SEG
    keys = ke.shape[0] - key_row
    win = ext - key_row
    heads_dim = width // HEADS
    sum_rows = qe.shape[0] - q_rows

    phase, shard = meta[0], meta[1]
    position = step - phase
    active = (position >= 0) & (position < micro)

    def fetch(source, target, index):
        pltpu.make_async_copy(source, target, xsem.at[index]).start()

    @pl.when(active)
    def _():
        names = (wk, wv, wq, wo, wp)
        own = xe.at[pl.ds(HALO, rows)]
        spots = []
        for distance, take in pieces:
            top = HALO - (distance - 1) * rows - take
            spots.append((distance, xe.at[pl.ds(top, take)]))
        if with_frames:
            @pl.when(phase == 0)
            def _():
                fetch(frames_hbm.at[step], own, 0)
                for n, (distance, spot) in enumerate(spots):
                    @pl.when(shard >= distance)
                    def _():
                        fetch(frame_halos[n].at[step], spot, 1 + n)
                    if step >= 1:
                        @pl.when(shard < distance)
                        def _():
                            fetch(frame_halos[n].at[step - 1], spot, 1 + n)
        if with_inbox:
            @pl.when(phase > 0)
            def _():
                fetch(inbox, own, 0)
                for n, (distance, spot) in enumerate(spots):
                    @pl.when(shard >= distance)
                    def _():
                        fetch(halos[n], spot, 1 + n)
                    if with_prev:
                        @pl.when((shard < distance) & (position > 0))
                        def _():
                            fetch(prevs[n], spot, 1 + n)
        for n, (source, target) in enumerate(zip(hbm_weights, names)):
            pltpu.make_async_copy(source, target, wsem.at[n]).start()
        pltpu.make_async_copy(taps_hbm, taps, wsem.at[5]).start()

        def need(n):
            if n == 5:
                pltpu.make_async_copy(taps_hbm, taps, wsem.at[5]).wait()
            else:
                pltpu.make_async_copy(hbm_weights[n], names[n], wsem.at[n]).wait()

        for n, (distance, spot) in enumerate(spots):
            @pl.when((shard < distance) & (position == 0))
            def _():
                spot[...] = jnp.zeros(spot.shape, jnp.bfloat16)

        first = position * segs_row + shard * (rows // SEG) - HALO_SEGS
        counts = []
        for s in range(segs):
            g = first + s
            safe = jnp.maximum(g, 0)
            value = counts_ref[safe // segs_row, safe % segs_row]
            counts.append(jnp.where(g >= 0, value, 0))

        row = lax.broadcasted_iota(jnp.int32, (q_rows, keys), 0)
        col = lax.broadcasted_iota(jnp.int32, (q_rows, keys), 1)
        line = lax.broadcasted_iota(jnp.int32, (1, keys), 1)
        kcount = by_segment(line // SEG, counts, key_seg, win // SEG)
        kvalid = (line % SEG) < kcount
        mvalid = by_segment(line - win, counts, mem_first, mems) > 0
        live = jnp.where((kvalid & (line < win)) | (mvalid & (line >= win)), 1, 0)
        segment = q_seg + row // SEG
        key_at = jnp.where(
            col < win, key_seg + col // SEG, mem_first + (col - win) + (BACK + 1000)
        )
        low = jnp.where(col < win, segment - BACK, segment - NMEM + (BACK + 1000))
        high = jnp.where(col < win, segment, segment - 1 + (BACK + 1000))
        good = (key_at >= low) & (key_at <= high) & (live > 0)
        bias[...] = jnp.where(good, OPEN, FAR)

        mem_keys = mem_bias.shape[1]
        mrow = lax.broadcasted_iota(jnp.int32, (mems * HEADS, mem_keys), 0)
        mcol = lax.broadcasted_iota(jnp.int32, (mems * HEADS, mem_keys), 1)
        mline = lax.broadcasted_iota(jnp.int32, (1, mem_keys), 1)
        mlive = (mline % SEG) < by_segment(mline // SEG, counts, 0, mem_keys // SEG)
        mseg = mem_first + mrow // HEADS
        mgood = (mcol // SEG >= mseg - BACK) & (mcol // SEG <= mseg) & mlive
        mem_bias[...] = jnp.where(mgood, OPEN, FAR)

        pltpu.make_async_copy(
            frames_hbm.at[step] if with_frames else inbox, own, xsem.at[0]
        ).wait()
        for n, (distance, spot) in enumerate(spots):
            @pl.when((shard >= distance) | (position > 0))
            def _():
                pltpu.make_async_copy(
                    frame_halos[n].at[step] if with_frames else halos[n], spot, xsem.at[1 + n]
                ).wait()
        for r in range(0, ext, SEG):
            part = xe[pl.ds(r, SEG), :].astype(jnp.float32)
            normed[pl.ds(r, SEG), :] = layer_norm(part).astype(jnp.bfloat16)

        def columns(n):
            return pl.ds(pl.multiple_of(n * TILE, TILE), TILE)

        need(0)

        @pl.loop(0, width // TILE)
        def _(n):
            at = columns(n)
            ke[pl.ds(0, ext), at] = dot(normed[...], wk[:, at]).astype(jnp.bfloat16)

        need(1)

        @pl.loop(0, width // TILE)
        def _(n):
            at = columns(n)
            ve[pl.ds(0, ext), at] = dot(normed[...], wv[:, at]).astype(jnp.bfloat16)

        srow = lax.broadcasted_iota(jnp.int32, (sum_rows, ext), 0)
        scol = lax.broadcasted_iota(jnp.int32, (sum_rows, ext), 1)
        sline = lax.broadcasted_iota(jnp.int32, (1, ext), 1)
        slive = (sline % SEG) < by_segment(sline // SEG, counts, 0, segs)
        pick = jnp.where((scol // SEG == srow + mem_first) & slive, 1.0, 0.0).astype(jnp.bfloat16)
        scount = by_segment(
            lax.broadcasted_iota(jnp.int32, (sum_rows, 1), 0), counts, mem_first, mems
        )
        divisor = jnp.maximum(scount, 1).astype(jnp.float32)
        summary = (dot(pick, normed[...]) / divisor).astype(jnp.bfloat16)

        scale = 1.0 / math.sqrt(heads_dim)
        need(2)

        @pl.loop(0, width // TILE)
        def _(n):
            at = columns(n)
            lhs = jnp.concatenate([normed[pl.ds(ext - q_rows, q_rows), :], summary])
            qe[:, at] = (dot(lhs, wq[:, at]) * scale).astype(jnp.bfloat16)

        head_of = lax.broadcasted_iota(jnp.int32, (HEADS, width), 1) // heads_dim
        own_head = head_of == lax.broadcasted_iota(jnp.int32, (HEADS, width), 0)
        sq = qe[pl.ds(q_rows, sum_rows), :].astype(jnp.float32)
        spread_q = []
        for m in range(mems):
            line_q = jnp.broadcast_to(sq[m : m + 1, :], (HEADS, width))
            spread_q.append(jnp.where(own_head, line_q, 0.0).astype(jnp.bfloat16))
        spread_q = jnp.concatenate(spread_q)
        ms = dot_nt(spread_q, ke[pl.ds(0, mem_keys), :])
        ms = jnp.minimum(ms, mem_bias[...])
        me = jnp.exp(ms - jnp.max(ms, axis=-1, keepdims=True))
        mw = (me / jnp.sum(me, axis=-1, keepdims=True)).astype(jnp.bfloat16)
        mo = dot(mw, ve[pl.ds(0, mem_keys), :])
        lines = []
        for m in range(mems):
            part = jnp.where(own_head, mo[m * HEADS : (m + 1) * HEADS, :], 0.0)
            lines.append(jnp.sum(part, axis=0, keepdims=True))
        lines.append(jnp.zeros((mem_pad - mems, width), jnp.float32))
        memory = jnp.concatenate(lines).astype(jnp.bfloat16)

        @pl.loop(0, width // TILE)
        def _(n):
            at = columns(n)
            ke[pl.ds(ext, mem_pad), at] = dot(memory, wk[:, at]).astype(jnp.bfloat16)
            ve[pl.ds(ext, mem_pad), at] = dot(memory, wv[:, at]).astype(jnp.bfloat16)

        lane = lax.broadcasted_iota(jnp.int32, (q_rows, PAIR), 1)
        even = lane < heads_dim

        @pl.loop(0, width // PAIR)
        def _(n):
            at = pl.ds(pl.multiple_of(n * PAIR, PAIR), PAIR)
            qp = qe[pl.ds(0, q_rows), at]
            zero = jnp.zeros_like(qp)
            kp = ke[pl.ds(key_row, keys), at]
            vp = ve[pl.ds(key_row, keys), at]
            halves = []
            for q_half in (jnp.where(even, qp, zero), jnp.where(even, zero, qp)):
                scores = jnp.minimum(dot_nt(q_half, kp), bias[...])
                weight = jnp.exp(scores - jnp.max(scores, axis=-1, keepdims=True))
                total = jnp.sum(weight, axis=-1, keepdims=True)
                halves.append(dot(weight.astype(jnp.bfloat16), vp) / total)
            ctx[:, at] = jnp.where(even, halves[0], halves[1]).astype(jnp.bfloat16)

        need(3)

        @pl.loop(0, width // TILE)
        def _(n):
            at = columns(n)
            x_part = xe[pl.ds(ext - q_rows, q_rows), at].astype(jnp.float32)
            res[:, at] = (x_part + dot(ctx[...], wo[:, at])).astype(jnp.bfloat16)

        inner = lax.broadcasted_iota(jnp.int32, (SEG, 1), 0)
        for s in range(q_rows // SEG):
            mask = (inner < counts[q_seg + s]).astype(jnp.float32)
            part = res[pl.ds(s * SEG, SEG), :].astype(jnp.float32)
            part = (layer_norm(part) * mask).astype(jnp.bfloat16)
            cin[pl.ds(s * SEG, SEG), :] = part.astype(jnp.float32)

        need(5)

        @pl.loop(0, width // PAIR)
        def _(n):
            at = pl.ds(pl.multiple_of(n * PAIR, PAIR), PAIR)
            total = jnp.zeros((rows, PAIR), jnp.float32)
            for j in range(KW):
                total = total + taps[pl.ds(j, 1), at] * cin[pl.ds(SEG - (KW - 1) + j, rows), at]
            depth[:, at] = total

        for r in range(0, rows, SEG):
            part = layer_norm(depth[pl.ds(r, SEG), :])
            gated[pl.ds(r, SEG), :] = (part / (1.0 + jnp.exp(-part))).astype(jnp.bfloat16)

        need(4)
        frame = lax.broadcasted_iota(jnp.int32, (rows, 1), 0)
        frame_ok = (frame % SEG) < by_segment(frame // SEG, counts, HALO_SEGS, rows // SEG)
        row_mask = frame_ok.astype(jnp.float32)

        @pl.loop(0, width // TILE)
        def _(n):
            at = columns(n)
            mixed = res[pl.ds(SEG, rows), at].astype(jnp.float32) + dot(gated[...], wp[:, at])
            result[:, at] = (mixed * row_mask).astype(jnp.bfloat16)

        copies = [pltpu.make_async_copy(result, outputs.at[position], osem.at[0])]
        if with_relay:
            copies.append(pltpu.make_async_copy(result, relays[0], osem.at[1]))
            spot = 1
            for _, take in pieces:
                if take < rows:
                    copies.append(
                        pltpu.make_async_copy(
                            result.at[pl.ds(rows - take, take)], relays[spot], osem.at[1 + spot]
                        )
                    )
                    spot += 1
        for copy in copies:
            copy.start()
        for copy in copies:
            copy.wait()


def per_device(frames, frame_counts, w_query, w_key, w_value, w_out, conv_kernel, w_point):
    micro, rows, width = frames.shape
    phases = lax.axis_size("phase")
    shards = lax.axis_size("tm")
    segs_row = frame_counts.shape[1]
    pieces = halo_pieces(rows)
    ext = HALO + rows
    q_rows = rows + SEG
    mems = ext // SEG - 1 - (HALO_SEGS - 1 - NMEM)
    mem_pad = -(-mems // SEG) * SEG
    sum_rows = -(-mems // 16) * 16
    mem_keys = (mems + BACK) * SEG
    keys = ext + mem_pad - (HALO_SEGS - 1 - BACK) * SEG

    meta = jnp.stack([lax.axis_index("phase"), lax.axis_index("tm")]).astype(jnp.int32)
    taps = jnp.pad(conv_kernel[0].astype(jnp.float32), ((0, 32 - KW), (0, 0)))

    frame_halos = []
    for distance, take in pieces:
        route = [(s * phases, (s + distance) % shards * phases) for s in range(shards)]
        frame_halos.append(
            lax.ppermute(frames[:, rows - take :, :], ("tm", "phase"), route)
        )

    def relay(blocks, step):
        senders = [p for p in range(phases - 1) if 0 <= step - p < micro]

        def send(block, distance):
            route = [
                (s * phases + p, (s + distance) % shards * phases + p + 1)
                for s in range(shards)
                for p in senders
            ]
            return lax.ppermute(block, ("tm", "phase"), route)

        got = [send(blocks[0], 0)]
        spot = 1
        for distance, take in pieces:
            if take < rows:
                got.append(send(blocks[spot], distance))
                spot += 1
            else:
                got.append(send(blocks[0], distance))
        return got

    def vmem(*shape, dtype=jnp.bfloat16):
        return pltpu.VMEM(shape, dtype)

    scratch = [
        vmem(ext, width), vmem(ext, width), vmem(ext + mem_pad, width), vmem(ext + mem_pad, width),
        vmem(q_rows + sum_rows, width), vmem(q_rows, width), vmem(q_rows, width),
        vmem(q_rows, width, dtype=jnp.float32), vmem(rows, width, dtype=jnp.float32),
        vmem(rows, width), vmem(rows, width),
        vmem(q_rows, keys, dtype=jnp.float32), vmem(mems * HEADS, mem_keys, dtype=jnp.float32),
        vmem(width, width), vmem(width, width), vmem(width, width), vmem(width, width),
        vmem(width, width), vmem(32, width, dtype=jnp.float32),
        pltpu.SemaphoreType.DMA((6,)),
        pltpu.SemaphoreType.DMA((1 + len(pieces),)),
        pltpu.SemaphoreType.DMA((2 + len(pieces),)),
    ]
    smem = pl.BlockSpec(memory_space=pltpu.SMEM)
    hbm = pl.BlockSpec(memory_space=pl.ANY)
    weights = [w_key[0], w_value[0], w_query[0], w_out[0], w_point[0]]
    block = jax.ShapeDtypeStruct((rows, width), jnp.bfloat16)
    tails = [
        jax.ShapeDtypeStruct((take, width), jnp.bfloat16) for _, take in pieces if take < rows
    ]
    whole = jax.ShapeDtypeStruct((micro, rows, width), jnp.bfloat16)

    outputs = None
    got, before = [], []
    steps = micro + phases - 1
    for step in range(steps):
        args = [meta, frame_counts, *weights, taps]
        if step < micro:
            args += [frames, *frame_halos]
        if step >= 1:
            args += got
        if step >= 2:
            args += before[1:]
        aliases = {}
        if step >= 1:
            aliases = {len(args): 0}
            args.append(outputs)
        last = step == steps - 1
        outs = [whole] if last else [whole, block, *tails]
        cfg = (rows, width, step, micro, phases, shards, segs_row, pieces)
        made = pl.pallas_call(
            functools.partial(layer_kernel, cfg),
            out_shape=outs,
            in_specs=[smem, smem] + [hbm] * (len(args) - 2),
            out_specs=[hbm] * len(outs),
            scratch_shapes=scratch,
            input_output_aliases=aliases,
            compiler_params=pltpu.CompilerParams(vmem_limit_bytes=48 * 1024 * 1024),
            name="layer",
        )(*args)
        outputs = made[0]
        if not last:
            before, got = got, relay(made[1:], step)
    return outputs[None]


def solution(mesh):
    in_specs = (
        P(None, "tm", None),
        P(),
        P("phase", None, None),
        P("phase", None, None),
        P("phase", None, None),
        P("phase", None, None),
        P("phase", None, None),
        P("phase", None, None),
    )
    out_specs = P("phase", None, "tm", None)
    return jax.shard_map(
        per_device, mesh=mesh, in_specs=in_specs, out_specs=out_specs, check_vma=False
    )
```

time: 391 us -> 163 us (0.42)
  the two profiles are of different devices: /device:TPU:1 before, /device:TPU:7 now
where the time goes in v1:
time: 163 us; the launch traced here: 162 us
  waiting for transfers between devices  102 us (63%)
  Pallas kernels  41.3 us (25%)
  starting transfers between devices  13.2 us (8%)
  local copies, waits for them, and re-layouts  4.34 us (3%)
    ppermute x12, waiting for transfers between devices, send(): return lax.ppermute(block, ('tm', 'phase'), route)  102 us
    pallas_call x5, Pallas kernels, per_device(): pl.pallas_call(functools.partial(layer_kernel, cfg), out_shape=outs, in_s...  41.3 us
    ppermute x12, starting transfers between devices, send(): return lax.ppermute(block, ('tm', 'phase'), route)  11.8 us
    unnamed x8, local copies, waits for them, and re-layouts  3.31 us
  transfers between devices with their start and end apart: 14, of which 2 were waited for; matrix products, arithmetic and copies ran while one was open for 1% of the time, Pallas kernels for 0%

profile of v1, /device:TPU:7, one launch (start us, length us, event | category | flops | bytes accessed | tf_op | source)
XLA Modules:
  0.0 162.3 jit_solution(18335063398235074148)
XLA Ops:
  0.0 0.7 collective-permute-start
  0.7 1.0 slice.3
  1.7 0.7 collective-permute-start.1
  2.4 0.1 pad_add_fusion.refs_0_
  2.5 0.8 pad_convert_fusion.refs_7_
  3.4 0.0 collective-permute-done.refs_9_
  3.4 0.0 copy-start
  3.4 1.6 copy-done
  5.0 1.0 copy-done.2
  6.0 0.7 copy-done.3
  6.7 0.7 layer.5
  7.4 0.7 collective-permute-start.3
  8.1 0.7 collective-permute-start.2
  8.7 0.7 collective-permute-start.4
  9.4 0.0 collective-permute-done.4.refs_13_.refs_12_
  9.4 0.0 collective-permute-done.3.refs_12_.refs_11_
  9.5 0.0 copy-start.1
  9.5 0.7 layer.6
  10.2 0.7 collective-permute-start.6
  10.8 0.7 collective-permute-start.5
  11.5 0.7 collective-permute-start.7
  12.3 0.9 layer.7
  13.2 1.3 collective-permute-start.9
  14.5 1.3 collective-permute-start.8
  15.8 1.3 collective-permute-start.10
  17.1 94.0 %collective-permute-done.10.refs_10_.refs_12_ = bf16[96,1024]{1,0:T(8,128)(2,1)S(1)} collective-permute-done((bf16[96,1024]{1,0:T(8,128)(2,1)S(1)}, bf16[96,1024]{1,0:T(8,128)(2,1)S(1)}, u32[]{:S(2)}, u32[]{:S(2)}) %collective-permute-start.10) | collective-permute-done | bytes 196640 | tf_op jit(solution)/shard_map/ppermute | solution.py:377
  111.1 19.4 %layer.8 = (bf16[2,128,1024]{2,1,0:T(8,128)(2,1)}, bf16[128,1024]{1,0:T(8,128)(2,1)S(1)}, bf16[96,1024]{1,0:T(8,128)(2,1)S(1)}) custom-call(s32[2]{0:T(128)S(1)} %pad_add_fusion.refs_0_, s32[2,32]{1,0:T(2,128)S(1)} %copy-done.3, bf16[1024,1024]{1,0:T(8,128)(2,1)S(1)} %bitcast.12, bf16[1024,1024]{1,0:T(8,128)(2,1)S(1)} %bitcast.17, ...), custom_call_target="tpu_custom_call", output_to_operand_aliasing={{0}: (13, {})} | custom-call | tf_op jit(solution)/shard_map/layer/pallas_call | solution.py:431
  130.5 1.3 collective-permute-start.12
  131.8 1.3 collective-permute-start.11
  133.1 1.3 collective-permute-start.13
  134.4 8.2 %collective-permute-done.13.refs_10_ = bf16[96,1024]{1,0:T(8,128)(2,1)S(1)} collective-permute-done((bf16[96,1024]{1,0:T(8,128)(2,1)S(1)}, bf16[96,1024]{1,0:T(8,128)(2,1)S(1)}, u32[]{:S(2)}, u32[]{:S(2)}) %collective-permute-start.13) | collective-permute-done | bytes 196640 | tf_op jit(solution)/shard_map/ppermute | solution.py:377
  142.5 19.6 %layer.9 = bf16[2,128,1024]{2,1,0:T(8,128)(2,1)} custom-call(s32[2]{0:T(128)S(1)} %pad_add_fusion.refs_0_, s32[2,32]{1,0:T(2,128)S(1)} %copy-done.3, bf16[1024,1024]{1,0:T(8,128)(2,1)S(1)} %bitcast.13, bf16[1024,1024]{1,0:T(8,128)(2,1)S(1)} %bitcast.18, bf16[1024,1024]{1,0:T(8,128)(2,1)} %bitcast.23, ...), custom_call_target="tpu_custom_call", output_to_operand_aliasing={{}: (13, {})} | custom-call | tf_op jit(solution)/shard_map/layer/pallas_call | solution.py:431
  (12 shorter events, 0.0 us)
Async XLA Ops:
  0.0 3.4 %collective-permute-start = (bf16[2,128,1024]{2,1,0:T(8,128)(2,1)}, bf16[2,128,1024]{2,1,0:T(8,128)(2,1)S(1)}, u32[]{:S(2)}, u32[]{:S(2)}) collective-permute-start(bf16[2,128,1024]{2,1,0:T(8,128)(2,1)} %refs_8_.3), channel_id=1, source_target_pairs={{0,4},{4,8},{8,12},{12,16},{16,20},{20,24},{24,28},{28,0}} | collective-permute-start | bytes 1572872 | tf_op jit(solution)/shard_map/ppermute | solution.py:365
  1.7 1.6 %collective-permute-start.1 = (bf16[2,96,1024]{2,1,0:T(8,128)(2,1)S(1)}, bf16[2,96,1024]{2,1,0:T(8,128)(2,1)S(1)}, u32[]{:S(2)}, u32[]{:S(2)}) collective-permute-start(bf16[2,96,1024]{2,1,0:T(8,128)(2,1)S(1)} %slice.3), channel_id=1, source_target_pairs={{0,8},{4,12},{8,16},{12,20},{16,24},{20,28},{24,0},{28,4}} | collective-permute-start | bytes 1179656 | tf_op jit(solution)/shard_map/ppermute | solution.py:365
  3.4 1.6 copy-start
  5.0 1.0 copy-start.2
  6.0 0.7 copy-start.3
  7.4 2.1 %collective-permute-start.3 = (bf16[128,1024]{1,0:T(8,128)(2,1)S(1)}, bf16[128,1024]{1,0:T(8,128)(2,1)S(1)}, u32[]{:S(2)}, u32[]{:S(2)}) collective-permute-start(bf16[128,1024]{1,0:T(8,128)(2,1)S(1)} %get-tuple-element.17), channel_id=1, source_target_pairs={{0,5},{4,9},{8,13},{12,17},{16,21},{20,25},{24,29},{28,1}} | collective-permute-start | bytes 786440 | tf_op jit(solution)/shard_map/ppermute | solution.py:377
  8.1 1.4 collective-permute-start.2
  8.7 0.7 collective-permute-start.4
  9.5 2.8 %copy-start.1 = (bf16[1,1024,1024]{2,1,0:T(8,128)(2,1)S(1)}, bf16[1,1024,1024]{2,1,0:T(8,128)(2,1)}, u32[]{:S(2)}) copy-start(bf16[1,1024,1024]{2,1,0:T(8,128)(2,1)} %param.12) | copy-start | bytes 6291460
  10.2 2.1 %collective-permute-start.6 = (bf16[128,1024]{1,0:T(8,128)(2,1)S(1)}, bf16[128,1024]{1,0:T(8,128)(2,1)S(1)}, u32[]{:S(2)}, u32[]{:S(2)}) collective-permute-start(bf16[128,1024]{1,0:T(8,128)(2,1)S(1)} %get-tuple-element.20), channel_id=1, source_target_pairs={{0,5},{1,6},{4,9},{5,10},{8,13},{9,14},{12,17},{13,18},{16,21},{17... | collective-permute-start | bytes 786440 | tf_op jit(solution)/shard_map/ppermute | solution.py:377
  10.8 1.4 collective-permute-start.5
  11.5 0.7 collective-permute-start.7
  13.2 97.9 %collective-permute-start.9 = (bf16[128,1024]{1,0:T(8,128)(2,1)S(1)}, bf16[128,1024]{1,0:T(8,128)(2,1)S(1)}, u32[]{:S(2)}, u32[]{:S(2)}) collective-permute-start(bf16[128,1024]{1,0:T(8,128)(2,1)S(1)} %get-tuple-element.23), channel_id=1, source_target_pairs={{1,6},{2,7},{5,10},{6,11},{9,14},{10,15},{13,18},{14,19},{17,22},{... | collective-permute-start | bytes 786440 | tf_op jit(solution)/shard_map/ppermute | solution.py:377
  14.5 96.6 %collective-permute-start.8 = (bf16[128,1024]{1,0:T(8,128)(2,1)S(1)}, bf16[128,1024]{1,0:T(8,128)(2,1)S(1)}, u32[]{:S(2)}, u32[]{:S(2)}) collective-permute-start(bf16[128,1024]{1,0:T(8,128)(2,1)S(1)} %get-tuple-element.23), channel_id=1, source_target_pairs={{1,2},{2,3},{5,6},{6,7},{9,10},{10,11},{13,14},{14,15},{17,18},{18... | collective-permute-start | bytes 786440 | tf_op jit(solution)/shard_map/ppermute | solution.py:377
  15.8 95.3 %collective-permute-start.10 = (bf16[96,1024]{1,0:T(8,128)(2,1)S(1)}, bf16[96,1024]{1,0:T(8,128)(2,1)S(1)}, u32[]{:S(2)}, u32[]{:S(2)}) collective-permute-start(bf16[96,1024]{1,0:T(8,128)(2,1)S(1)} %get-tuple-element.24), channel_id=1, source_target_pairs={{1,10},{2,11},{5,14},{6,15},{9,18},{10,19},{13,22},{14,23},{17,26}... | collective-permute-start | bytes 589832 | tf_op jit(solution)/shard_map/ppermute | solution.py:377
  130.5 12.1 %collective-permute-start.12 = (bf16[128,1024]{1,0:T(8,128)(2,1)S(1)}, bf16[128,1024]{1,0:T(8,128)(2,1)S(1)}, u32[]{:S(2)}, u32[]{:S(2)}) collective-permute-start(bf16[128,1024]{1,0:T(8,128)(2,1)S(1)} %get-tuple-element.26), channel_id=1, source_target_pairs={{2,7},{6,11},{10,15},{14,19},{18,23},{22,27},{26,31},{30,3}} | collective-permute-start | bytes 786440 | tf_op jit(solution)/shard_map/ppermute | solution.py:377
  131.8 10.8 %collective-permute-start.11 = (bf16[128,1024]{1,0:T(8,128)(2,1)S(1)}, bf16[128,1024]{1,0:T(8,128)(2,1)S(1)}, u32[]{:S(2)}, u32[]{:S(2)}) collective-permute-start(bf16[128,1024]{1,0:T(8,128)(2,1)S(1)} %get-tuple-element.26), channel_id=1, source_target_pairs={{2,3},{6,7},{10,11},{14,15},{18,19},{22,23},{26,27},{30,31}} | collective-permute-start | bytes 786440 | tf_op jit(solution)/shard_map/ppermute | solution.py:377
  133.1 9.5 %collective-permute-start.13 = (bf16[96,1024]{1,0:T(8,128)(2,1)S(1)}, bf16[96,1024]{1,0:T(8,128)(2,1)S(1)}, u32[]{:S(2)}, u32[]{:S(2)}) collective-permute-start(bf16[96,1024]{1,0:T(8,128)(2,1)S(1)} %get-tuple-element.27), channel_id=1, source_target_pairs={{2,11},{6,15},{10,19},{14,23},{18,27},{22,31},{26,3},{30,7}} | collective-permute-start | bytes 589832 | tf_op jit(solution)/shard_map/ppermute | solution.py:377
